TPU v7x, 512 devices: a whole 4x4x16 slice. The times are simulated.
512 devices in a mesh: mem: 8 (over y, core), grid: 64 (over x, z).
Axes of the slice: x: 4, y: 4, z: 16, core: 2. Of those that a mesh axis runs over, the one named last changes fastest.
Arguments:
- ensemble: bfloat16 [80, 160, 16384], P('mem', None, 'grid'), may hold values from -6 to 6
- obs_prior: bfloat16 [80, 1048576], P(None, ('mem', 'grid')), may hold values from -15 to 15
- obs_value: bfloat16 [1048576], P(('mem', 'grid')), may hold values from -8 to 8
- obs_precision: bfloat16 [1048576], P(('mem', 'grid')), may hold values from 0.049804688 to 1
- entry_ids: int32 [8, 64, 2, 512], P('mem', 'grid'), may hold values from 0 to 131071, as said below
- entry_count: int32 [8, 64, 2], P('mem', 'grid'), may hold values from 1 to 512, as said below
- entry_taper: float32 [8, 64, 2, 512], P('mem', 'grid'), may hold values from 0.05 to 1
Outputs:
- analysis: bfloat16 [80, 160, 16384], P('mem', None, 'grid')
Inputs may be any that keep to these rules, and one draw needn't show every extreme that they name: `entry_ids`: on the devices of mem index m and grid index g, an entry id names observation m * 64 * 2048 + id, held by grid index id // 2048 at row id % 2048. That grid index is g or lies within 4 grid indices of g, counted cyclically. Among one device's 2 * 512 entries at most 128 name any one grid index other than g, and on every device some grid index is named exactly 128 times. `entry_count`: some list is full.
All inputs are finite; a program needn't handle non-finite values.
Results may differ from a plain program's by a relative error of at most 0.0057.
Values may be sent and summed in bfloat16 or wider, within the bound.
A program may use at most 64 MiB of HBM per device.

v0:
```python
import jax
import jax.numpy as jnp
from jax import lax
from jax.sharding import PartitionSpec as P

BLOCK = 128
REACH = 4
ITERS = 5


highest = lax.Precision.HIGHEST


def from_behind(block, axis, distance):
    devices = range(lax.axis_size(axis))
    route = [((i - distance) % len(devices), i) for i in devices]
    return lax.ppermute(block, axis, route)


def block_transform(gram, drive):
    members = gram.shape[-1]
    identity = jnp.eye(members, dtype=jnp.float32)
    system = gram + (members - 1.0) * identity
    scale = jnp.sqrt(jnp.sum(system * system, axis=(1, 2)))
    root_iter = system / scale[:, None, None]
    inverse_root = jnp.broadcast_to(identity, system.shape)
    for sweep_index in range(ITERS):
        update = 1.5 * identity - 0.5 * jnp.einsum(
            "bij,bjk->bik", inverse_root, root_iter, precision=highest
        )
        root_iter = jnp.einsum("bij,bjk->bik", root_iter, update, precision=highest)
        inverse_root = jnp.einsum("bij,bjk->bik", update, inverse_root, precision=highest)
    spread = jnp.sqrt((members - 1.0) / scale)[:, None, None] * inverse_root
    inner_step = jnp.einsum("bij,bj->bi", inverse_root, drive, precision=highest)
    mean_shift = (
        jnp.einsum("bij,bj->bi", inverse_root, inner_step, precision=highest) / scale[:, None]
    )
    return spread + mean_shift[:, :, None]


def body(ensemble, obs_prior, obs_value, obs_precision, entry_ids, entry_count, entry_taper):
    members = ensemble.shape[0] * lax.axis_size("mem")
    states = lax.all_to_all(ensemble, "mem", split_axis=1, concat_axis=0, tiled=True)
    local_rows = obs_prior.shape[1]
    details_local = jnp.stack([obs_value, obs_precision])
    flat_ids = entry_ids.reshape(-1)
    grid_index = lax.axis_index("grid")
    grid_count = lax.axis_size("grid")
    holder = flat_ids // local_rows
    row_index = flat_ids % local_rows
    prior_parts = []
    info_parts = []
    for offset in range(-REACH, REACH + 1):
        if offset == 0:
            prior_parts.append(obs_prior)
            info_parts.append(details_local)
        else:
            near_prior, near_info = from_behind((obs_prior, details_local), "grid", -offset)
            prior_parts.append(near_prior)
            info_parts.append(near_info)
    prior_table = jnp.concatenate(prior_parts, axis=1)
    info_table = jnp.concatenate(info_parts, axis=1)
    slot_index = (holder - grid_index + REACH) % grid_count
    lookup = slot_index * local_rows + row_index
    columns = jnp.take(prior_table, lookup, axis=1).astype(jnp.float32)
    details = jnp.take(info_table, lookup, axis=1).astype(jnp.float32)
    center = jnp.mean(columns, axis=0)
    deviation = columns - center
    innovation = details[0] - center
    blocks = entry_ids.shape[2]
    per_block = entry_ids.shape[3]
    valid_mask = (
        jnp.arange(per_block, dtype=jnp.int32)[None, :] < entry_count.reshape(blocks, 1)
    ).reshape(-1)
    weights = jnp.where(valid_mask, entry_taper.reshape(-1) * details[1], 0.0)
    shaped = deviation.reshape(members, blocks, per_block)
    weighted = (deviation * weights).reshape(members, blocks, per_block)
    gram_local = jnp.einsum("kbj,lbj->bkl", weighted, shaped, precision=highest)
    driven = (weights * innovation).reshape(blocks, per_block)
    drive_local = jnp.einsum("kbj,bj->bk", shaped, driven, precision=highest)
    gram_total, drive_total = lax.psum((gram_local, drive_local), "mem")
    transform = block_transform(gram_total, drive_total).astype(jnp.bfloat16)
    level_count = states.shape[1]
    column_count = states.shape[2]
    center_states = jnp.mean(states, axis=0, dtype=jnp.float32)
    anomalies = (states.astype(jnp.float32) - center_states).astype(jnp.bfloat16)
    anomalies = anomalies.reshape(members, level_count, blocks, BLOCK)
    analysed = jnp.einsum(
        "jvbc,bjk->kvbc", anomalies, transform, preferred_element_type=jnp.float32
    )
    analysed = (analysed + center_states.reshape(level_count, blocks, BLOCK)).astype(jnp.bfloat16)
    analysed = analysed.reshape(members, level_count, column_count)
    return lax.all_to_all(analysed, "mem", split_axis=0, concat_axis=1, tiled=True)


def solution(mesh):
    return jax.shard_map(
        body,
        mesh=mesh,
        in_specs=(
            P("mem", None, "grid"),
            P(None, ("mem", "grid")),
            P(("mem", "grid")),
            P(("mem", "grid")),
            P("mem", "grid", None, None),
            P("mem", "grid", None),
            P("mem", "grid", None, None),
        ),
        out_specs=P("mem", None, "grid"),
        check_vma=False,
    )
```

profile of v0, /device:TPU:32, one launch (start us, length us, event | category | flops | bytes accessed | tf_op | source)
XLA Modules:
  0.0 289.0 jit_solution(2944921145853714896)
XLA Ops:
  0.0 0.7 stack.10
  1.5 9.1 %collective-permute-start.8 = (bf16[2,2048]{1,0:T(2,128)(2,1)S(1)}, bf16[2,2048]{1,0:T(2,128)(2,1)S(1)}, u32[]{:S(2)}, u32[]{:S(2)}) collective-permute-start(bf16[2,2048]{1,0:T(2,128)(2,1)S(1)} %pad_maximum_fusion), channel_id=1, source_target_pairs={{60,0},{61,1},{62,2},{63,3},{0,4},{1,5},{2,6},{3,7},{4,8},{5,9},{6... | collective-permute-start | bytes 24584 | tf_op jit(solution)/shard_map/ppermute | solution.py:17
  10.6 7.7 %collective-permute-start.9 = (bf16[2,2048]{1,0:T(2,128)(2,1)S(1)}, bf16[2,2048]{1,0:T(2,128)(2,1)S(1)}, u32[]{:S(2)}, u32[]{:S(2)}) collective-permute-start(bf16[2,2048]{1,0:T(2,128)(2,1)S(1)} %pad_maximum_fusion), channel_id=1, source_target_pairs={{61,0},{62,1},{63,2},{0,3},{1,4},{2,5},{3,6},{4,7},{5,8},{6,9},{7,... | collective-permute-start | bytes 24584 | tf_op jit(solution)/shard_map/ppermute | solution.py:17
  18.3 3.4 %collective-permute-start.10 = (bf16[2,2048]{1,0:T(2,128)(2,1)S(1)}, bf16[2,2048]{1,0:T(2,128)(2,1)S(1)}, u32[]{:S(2)}, u32[]{:S(2)}) collective-permute-start(bf16[2,2048]{1,0:T(2,128)(2,1)S(1)} %pad_maximum_fusion), channel_id=1, source_target_pairs={{62,0},{63,1},{0,2},{1,3},{2,4},{3,5},{4,6},{5,7},{6,8},{7,9},{8,1... | collective-permute-start | bytes 24584 | tf_op jit(solution)/shard_map/ppermute | solution.py:17
  21.7 2.9 %collective-permute-start.11 = (bf16[2,2048]{1,0:T(2,128)(2,1)S(1)}, bf16[2,2048]{1,0:T(2,128)(2,1)S(1)}, u32[]{:S(2)}, u32[]{:S(2)}) collective-permute-start(bf16[2,2048]{1,0:T(2,128)(2,1)S(1)} %pad_maximum_fusion), channel_id=1, source_target_pairs={{63,0},{0,1},{1,2},{2,3},{3,4},{4,5},{5,6},{6,7},{7,8},{8,9},{9,10... | collective-permute-start | bytes 24584 | tf_op jit(solution)/shard_map/ppermute | solution.py:17
  24.7 2.9 %collective-permute-start.12 = (bf16[2,2048]{1,0:T(2,128)(2,1)S(1)}, bf16[2,2048]{1,0:T(2,128)(2,1)}, u32[]{:S(2)}, u32[]{:S(2)}) collective-permute-start(bf16[2,2048]{1,0:T(2,128)(2,1)S(1)} %pad_maximum_fusion), channel_id=1, source_target_pairs={{1,0},{2,1},{3,2},{4,3},{5,4},{6,5},{7,6},{8,7},{9,8},{10,9},{11,1... | collective-permute-start | bytes 24584 | tf_op jit(solution)/shard_map/ppermute | solution.py:17
  27.6 2.7 copy.53
  30.3 4.5 %all-to-all-start = ((bf16[10,160,256]{2,0,1:T(8,128)(2,1)}), bf16[10,160,256]{2,0,1:T(8,128)(2,1)S(1)}, u32[]{:S(2)}, u32[]{:S(2)}) async-start(bf16[10,160,256]{2,0,1:T(8,128)(2,1)} %copy.53), calls=%async_computation | async-start | bytes 2621440 | tf_op jit(solution)/shard_map/all_to_all | solution.py:43
  35.7 0.9 copy.78
  37.1 6.7 %collective-permute-start.13 = (bf16[2,2048]{1,0:T(2,128)(2,1)S(1)}, bf16[2,2048]{1,0:T(2,128)(2,1)S(1)}, u32[]{:S(2)}, u32[]{:S(2)}) collective-permute-start(bf16[2,2048]{1,0:T(2,128)(2,1)S(1)} %pad_maximum_fusion), channel_id=1, source_target_pairs={{2,0},{3,1},{4,2},{5,3},{6,4},{7,5},{8,6},{9,7},{10,8},{11,9},{12,... | collective-permute-start | bytes 24584 | tf_op jit(solution)/shard_map/ppermute | solution.py:17
  44.4 1.9 collective-permute-start.14
  46.9 4.8 %collective-permute-start.15 = (bf16[2,2048]{1,0:T(2,128)(2,1)S(1)}, bf16[2,2048]{1,0:T(2,128)(2,1)S(1)}, u32[]{:S(2)}, u32[]{:S(2)}) collective-permute-start(bf16[2,2048]{1,0:T(2,128)(2,1)S(1)} %pad_maximum_fusion), channel_id=1, source_target_pairs={{4,0},{5,1},{6,2},{7,3},{8,4},{9,5},{10,6},{11,7},{12,8},{13,9},{1... | collective-permute-start | bytes 24584 | tf_op jit(solution)/shard_map/ppermute | solution.py:17
  52.4 4.9 %collective-permute-start = (bf16[80,2048]{0,1:T(8,128)(2,1)S(1)}, bf16[80,2048]{0,1:T(8,128)(2,1)S(1)}, u32[]{:S(2)}, u32[]{:S(2)}) collective-permute-start(bf16[80,2048]{0,1:T(8,128)(2,1)S(1)} %copy.40), channel_id=1, source_target_pairs={{60,0},{61,1},{62,2},{63,3},{0,4},{1,5},{2,6},{3,7},{4,8},{5,9},{6... | collective-permute-start | bytes 983048 | tf_op jit(solution)/shard_map/ppermute | solution.py:17
  58.5 6.9 %collective-permute-start.1 = (bf16[80,2048]{0,1:T(8,128)(2,1)S(1)}, bf16[80,2048]{0,1:T(8,128)(2,1)S(1)}, u32[]{:S(2)}, u32[]{:S(2)}) collective-permute-start(bf16[80,2048]{0,1:T(8,128)(2,1)S(1)} %copy.40), channel_id=1, source_target_pairs={{61,0},{62,1},{63,2},{0,3},{1,4},{2,5},{3,6},{4,7},{5,8},{6,9},{7,... | collective-permute-start | bytes 983048 | tf_op jit(solution)/shard_map/ppermute | solution.py:17
  65.5 1.3 constant_dynamic-update-slice_fusion.12
  66.8 1.9 collective-permute-start.2
  69.3 2.9 %collective-permute-start.3 = (bf16[80,2048]{0,1:T(8,128)(2,1)S(1)}, bf16[80,2048]{0,1:T(8,128)(2,1)}, u32[]{:S(2)}, u32[]{:S(2)}) collective-permute-start(bf16[80,2048]{0,1:T(8,128)(2,1)S(1)} %copy.40), channel_id=1, source_target_pairs={{63,0},{0,1},{1,2},{2,3},{3,4},{4,5},{5,6},{6,7},{7,8},{8,9},{9,10... | collective-permute-start | bytes 983048 | tf_op jit(solution)/shard_map/ppermute | solution.py:17
  72.8 3.4 %collective-permute-start.4 = (bf16[80,2048]{0,1:T(8,128)(2,1)S(1)}, bf16[80,2048]{0,1:T(8,128)(2,1)}, u32[]{:S(2)}, u32[]{:S(2)}) collective-permute-start(bf16[80,2048]{0,1:T(8,128)(2,1)S(1)} %copy.40), channel_id=1, source_target_pairs={{1,0},{2,1},{3,2},{4,3},{5,4},{6,5},{7,6},{8,7},{9,8},{10,9},{11,1... | collective-permute-start | bytes 983048 | tf_op jit(solution)/shard_map/ppermute | solution.py:17
  76.8 4.4 %copy.50 = bf16[2,18432]{0,1:T(8,128)(2,1)} copy(bf16[2,18432]{1,0:T(2,128)(2,1)} %constant_dynamic-update-slice_fusion.9) | data formatting | bytes 147456 | tf_op jit(solution)/shard_map/concatenate | solution.py:62
  81.2 7.0 %gather_fusion.1 = bf16[1024,2]{1,0:T(8,128)(2,1)} fusion(bf16[2,18432]{0,1:T(8,128)(2,1)} %copy.50, s32[1024]{0:T(1024)S(1)} %broadcast_clamp_fusion), kind=kCustom, calls=%fused_computation.1 | custom fusion | bytes 12288 | tf_op jit(solution)/shard_map/jit(_take)/gather | solution.py:66
  88.2 1.2 convert_bitcast_fusion
  89.4 1.5 slice_reduce_fusion
  91.0 2.8 collective-permute-done
  93.8 21.4 %collective-permute-start.5 = (bf16[80,2048]{0,1:T(8,128)(2,1)S(1)}, bf16[80,2048]{0,1:T(8,128)(2,1)S(1)}, u32[]{:S(2)}, u32[]{:S(2)}) collective-permute-start(bf16[80,2048]{0,1:T(8,128)(2,1)S(1)} %copy.40), channel_id=1, source_target_pairs={{2,0},{3,1},{4,2},{5,3},{6,4},{7,5},{8,6},{9,7},{10,8},{11,9},{12,... | collective-permute-start | bytes 983048 | tf_op jit(solution)/shard_map/ppermute | solution.py:17
  115.2 0.8 constant_dynamic-update-slice_fusion.8
  116.0 24.2 %collective-permute-done.1 = bf16[80,2048]{0,1:T(8,128)(2,1)S(1)} collective-permute-done((bf16[80,2048]{0,1:T(8,128)(2,1)S(1)}, bf16[80,2048]{0,1:T(8,128)(2,1)S(1)}, u32[]{:S(2)}, u32[]{:S(2)}) %collective-permute-start.1) | collective-permute-done | bytes 327712 | tf_op jit(solution)/shard_map/ppermute | solution.py:17
  140.2 4.6 %collective-permute-start.6 = (bf16[80,2048]{0,1:T(8,128)(2,1)S(1)}, bf16[80,2048]{0,1:T(8,128)(2,1)S(1)}, u32[]{:S(2)}, u32[]{:S(2)}) collective-permute-start(bf16[80,2048]{0,1:T(8,128)(2,1)S(1)} %copy.40), channel_id=1, source_target_pairs={{3,0},{4,1},{5,2},{6,3},{7,4},{8,5},{9,6},{10,7},{11,8},{12,9},{13... | collective-permute-start | bytes 983048 | tf_op jit(solution)/shard_map/ppermute | solution.py:17
  144.9 0.8 constant_dynamic-update-slice_fusion.7
  145.7 16.2 %collective-permute-done.2 = bf16[80,2048]{0,1:T(8,128)(2,1)} collective-permute-done((bf16[80,2048]{0,1:T(8,128)(2,1)S(1)}, bf16[80,2048]{0,1:T(8,128)(2,1)}, u32[]{:S(2)}, u32[]{:S(2)}) %collective-permute-start.2) | collective-permute-done | bytes 327712 | tf_op jit(solution)/shard_map/ppermute | solution.py:17
  161.9 5.2 %collective-permute-start.7 = (bf16[80,2048]{0,1:T(8,128)(2,1)S(1)}, bf16[80,2048]{0,1:T(8,128)(2,1)S(1)}, u32[]{:S(2)}, u32[]{:S(2)}) collective-permute-start(bf16[80,2048]{0,1:T(8,128)(2,1)S(1)} %copy.40), channel_id=1, source_target_pairs={{4,0},{5,1},{6,2},{7,3},{8,4},{9,5},{10,6},{11,7},{12,8},{13,9},{1... | collective-permute-start | bytes 983048 | tf_op jit(solution)/shard_map/ppermute | solution.py:17
  167.1 1.9 constant_dynamic-update-slice_fusion.6
  168.9 1.5 collective-permute-done.3
  170.4 1.9 constant_dynamic-update-slice_fusion.5
  172.3 0.8 constant_dynamic-update-slice_fusion.4
  173.2 1.9 constant_dynamic-update-slice_fusion.3
  175.0 0.8 constant_dynamic-update-slice_fusion.2
  175.9 15.4 %collective-permute-done.6 = bf16[80,2048]{0,1:T(8,128)(2,1)S(1)} collective-permute-done((bf16[80,2048]{0,1:T(8,128)(2,1)S(1)}, bf16[80,2048]{0,1:T(8,128)(2,1)S(1)}, u32[]{:S(2)}, u32[]{:S(2)}) %collective-permute-start.6) | collective-permute-done | bytes 327712 | tf_op jit(solution)/shard_map/ppermute | solution.py:17
  191.3 0.8 constant_dynamic-update-slice_fusion.1
  192.1 31.9 %collective-permute-done.7 = bf16[80,2048]{0,1:T(8,128)(2,1)S(1)} collective-permute-done((bf16[80,2048]{0,1:T(8,128)(2,1)S(1)}, bf16[80,2048]{0,1:T(8,128)(2,1)S(1)}, u32[]{:S(2)}, u32[]{:S(2)}) %collective-permute-start.7) | collective-permute-done | bytes 327712 | tf_op jit(solution)/shard_map/ppermute | solution.py:17
  224.1 0.8 constant_dynamic-update-slice_fusion
  224.9 5.8 %gather_fusion = bf16[1024,80]{1,0:T(8,128)(2,1)S(1)} fusion(bf16[80,18432]{0,1:T(8,128)(2,1)} %constant_dynamic-update-slice_fusion, s32[1024]{0:T(1024)S(1)} %broadcast_clamp_fusion), kind=kCustom, calls=%fused_computation | custom fusion | bytes 331776 | tf_op jit(solution)/shard_map/jit(_take)/gather | solution.py:65
  232.3 26.4 %all-reduce = (f32[2,80,80]{2,1,0:T(8,128)S(1)}, f32[2,80]{1,0:T(2,128)S(1)}) all-reduce(f32[2,80,80]{2,1,0:T(8,128)S(1)} %fusion.11, f32[2,80]{1,0:T(2,128)S(1)} %bitcast.129), channel_id=1, replica_groups=mesh['mem'=8,'grid'=64] {'mem'}, use_global_device_ids=true, to_apply=%region_1.2 | all-reduce | flops 12960 | bytes 103680 | tf_op jit(solution)/shard_map/psum | solution.py:81
  262.9 1.0 copy.55
  263.9 2.0 reshape.285
  266.6 2.0 fusion
  268.6 0.8 copy.73
  270.0 17.8 %all_to_all.27 = bf16[80,20,256]{2,1,0:T(8,128)(2,1)S(1)} all-to-all(bf16[80,20,256]{2,1,0:T(8,128)(2,1)S(1)} %reshape.311), channel_id=1, replica_groups=mesh['mem'=8,'grid'=64] {'mem'}, dimensions={0} | all-to-all | bytes 1638400 | tf_op jit(solution)/shard_map/all_to_all | solution.py:93
  287.9 1.1 all_to_all.24
  (88 shorter events, 13.9 us)
Async XLA Ops:
  0.0 34.8 %copy-start.1 = (s32[1,1,2,512]{3,2,1,0:T(2,128)S(1)}, s32[1,1,2,512]{3,2,1,0:T(2,128)}, u32[]{:S(2)}) copy-start(s32[1,1,2,512]{3,2,1,0:T(2,128)} %param.11) | copy-start | bytes 12292
  0.0 35.6 %copy-start.6 = (s32[1,1,2]{2,1,0:T(1,128)S(1)}, s32[1,1,2]{2,1,0:T(1,128)}, u32[]{:S(2)}) copy-start(s32[1,1,2]{2,1,0:T(1,128)} %param.12) | copy-start | bytes 28
  0.0 36.6 %copy-start.2 = (f32[1,1,2,512]{3,2,1,0:T(2,128)S(1)}, f32[1,1,2,512]{3,2,1,0:T(2,128)}, u32[]{:S(2)}) copy-start(f32[1,1,2,512]{3,2,1,0:T(2,128)} %param.13) | copy-start | bytes 12292
  0.0 36.8 %copy-start = (bf16[80,2048]{1,0:T(8,128)(2,1)S(1)}, bf16[80,2048]{1,0:T(8,128)(2,1)}, u32[]{:S(2)}) copy-start(bf16[80,2048]{1,0:T(8,128)(2,1)} %param.8) | copy-start | bytes 983044
  1.5 35.6 %collective-permute-start.8 = (bf16[2,2048]{1,0:T(2,128)(2,1)S(1)}, bf16[2,2048]{1,0:T(2,128)(2,1)S(1)}, u32[]{:S(2)}, u32[]{:S(2)}) collective-permute-start(bf16[2,2048]{1,0:T(2,128)(2,1)S(1)} %pad_maximum_fusion), channel_id=1, source_target_pairs={{60,0},{61,1},{62,2},{63,3},{0,4},{1,5},{2,6},{3,7},{4,8},{5,9},{6... | collective-permute-start | bytes 24584 | tf_op jit(solution)/shard_map/ppermute | solution.py:17
  10.6 33.8 %collective-permute-start.9 = (bf16[2,2048]{1,0:T(2,128)(2,1)S(1)}, bf16[2,2048]{1,0:T(2,128)(2,1)S(1)}, u32[]{:S(2)}, u32[]{:S(2)}) collective-permute-start(bf16[2,2048]{1,0:T(2,128)(2,1)S(1)} %pad_maximum_fusion), channel_id=1, source_target_pairs={{61,0},{62,1},{63,2},{0,3},{1,4},{2,5},{3,6},{4,7},{5,8},{6,9},{7,... | collective-permute-start | bytes 24584 | tf_op jit(solution)/shard_map/ppermute | solution.py:17
  18.3 28.6 %collective-permute-start.10 = (bf16[2,2048]{1,0:T(2,128)(2,1)S(1)}, bf16[2,2048]{1,0:T(2,128)(2,1)S(1)}, u32[]{:S(2)}, u32[]{:S(2)}) collective-permute-start(bf16[2,2048]{1,0:T(2,128)(2,1)S(1)} %pad_maximum_fusion), channel_id=1, source_target_pairs={{62,0},{63,1},{0,2},{1,3},{2,4},{3,5},{4,6},{5,7},{6,8},{7,9},{8,1... | collective-permute-start | bytes 24584 | tf_op jit(solution)/shard_map/ppermute | solution.py:17
  21.7 30.7 %collective-permute-start.11 = (bf16[2,2048]{1,0:T(2,128)(2,1)S(1)}, bf16[2,2048]{1,0:T(2,128)(2,1)S(1)}, u32[]{:S(2)}, u32[]{:S(2)}) collective-permute-start(bf16[2,2048]{1,0:T(2,128)(2,1)S(1)} %pad_maximum_fusion), channel_id=1, source_target_pairs={{63,0},{0,1},{1,2},{2,3},{3,4},{4,5},{5,6},{6,7},{7,8},{8,9},{9,10... | collective-permute-start | bytes 24584 | tf_op jit(solution)/shard_map/ppermute | solution.py:17
  24.7 33.9 %collective-permute-start.12 = (bf16[2,2048]{1,0:T(2,128)(2,1)S(1)}, bf16[2,2048]{1,0:T(2,128)(2,1)}, u32[]{:S(2)}, u32[]{:S(2)}) collective-permute-start(bf16[2,2048]{1,0:T(2,128)(2,1)S(1)} %pad_maximum_fusion), channel_id=1, source_target_pairs={{1,0},{2,1},{3,2},{4,3},{5,4},{6,5},{7,6},{8,7},{9,8},{10,9},{11,1... | collective-permute-start | bytes 24584 | tf_op jit(solution)/shard_map/ppermute | solution.py:17
  30.3 232.2 %all-to-all-start = ((bf16[10,160,256]{2,0,1:T(8,128)(2,1)}), bf16[10,160,256]{2,0,1:T(8,128)(2,1)S(1)}, u32[]{:S(2)}, u32[]{:S(2)}) async-start(bf16[10,160,256]{2,0,1:T(8,128)(2,1)} %copy.53), calls=%async_computation | async-start | bytes 2621440 | tf_op jit(solution)/shard_map/all_to_all | solution.py:43
  35.6 52.7 %copy-start.3 = (pred[1024]{0:T(1024)(128)(4,1)}, pred[1024]{0:T(1024)(128)(4,1)S(1)}, u32[]{:S(2)}) copy-start(pred[1024]{0:T(1024)(128)(4,1)S(1)} %compare_and_fusion.1) | copy-start | bytes 3076
  37.1 29.7 %collective-permute-start.13 = (bf16[2,2048]{1,0:T(2,128)(2,1)S(1)}, bf16[2,2048]{1,0:T(2,128)(2,1)S(1)}, u32[]{:S(2)}, u32[]{:S(2)}) collective-permute-start(bf16[2,2048]{1,0:T(2,128)(2,1)S(1)} %pad_maximum_fusion), channel_id=1, source_target_pairs={{2,0},{3,1},{4,2},{5,3},{6,4},{7,5},{8,6},{9,7},{10,8},{11,9},{12,... | collective-permute-start | bytes 24584 | tf_op jit(solution)/shard_map/ppermute | solution.py:17
  44.4 24.9 %collective-permute-start.14 = (bf16[2,2048]{1,0:T(2,128)(2,1)S(1)}, bf16[2,2048]{1,0:T(2,128)(2,1)S(1)}, u32[]{:S(2)}, u32[]{:S(2)}) collective-permute-start(bf16[2,2048]{1,0:T(2,128)(2,1)S(1)} %pad_maximum_fusion), channel_id=1, source_target_pairs={{3,0},{4,1},{5,2},{6,3},{7,4},{8,5},{9,6},{10,7},{11,8},{12,9},{13... | collective-permute-start | bytes 24584 | tf_op jit(solution)/shard_map/ppermute | solution.py:17
  46.9 25.9 %collective-permute-start.15 = (bf16[2,2048]{1,0:T(2,128)(2,1)S(1)}, bf16[2,2048]{1,0:T(2,128)(2,1)S(1)}, u32[]{:S(2)}, u32[]{:S(2)}) collective-permute-start(bf16[2,2048]{1,0:T(2,128)(2,1)S(1)} %pad_maximum_fusion), channel_id=1, source_target_pairs={{4,0},{5,1},{6,2},{7,3},{8,4},{9,5},{10,6},{11,7},{12,8},{13,9},{1... | collective-permute-start | bytes 24584 | tf_op jit(solution)/shard_map/ppermute | solution.py:17
  52.4 41.4 %collective-permute-start = (bf16[80,2048]{0,1:T(8,128)(2,1)S(1)}, bf16[80,2048]{0,1:T(8,128)(2,1)S(1)}, u32[]{:S(2)}, u32[]{:S(2)}) collective-permute-start(bf16[80,2048]{0,1:T(8,128)(2,1)S(1)} %copy.40), channel_id=1, source_target_pairs={{60,0},{61,1},{62,2},{63,3},{0,4},{1,5},{2,6},{3,7},{4,8},{5,9},{6... | collective-permute-start | bytes 983048 | tf_op jit(solution)/shard_map/ppermute | solution.py:17
  58.5 81.7 %collective-permute-start.1 = (bf16[80,2048]{0,1:T(8,128)(2,1)S(1)}, bf16[80,2048]{0,1:T(8,128)(2,1)S(1)}, u32[]{:S(2)}, u32[]{:S(2)}) collective-permute-start(bf16[80,2048]{0,1:T(8,128)(2,1)S(1)} %copy.40), channel_id=1, source_target_pairs={{61,0},{62,1},{63,2},{0,3},{1,4},{2,5},{3,6},{4,7},{5,8},{6,9},{7,... | collective-permute-start | bytes 983048 | tf_op jit(solution)/shard_map/ppermute | solution.py:17
  66.8 95.1 %collective-permute-start.2 = (bf16[80,2048]{0,1:T(8,128)(2,1)S(1)}, bf16[80,2048]{0,1:T(8,128)(2,1)}, u32[]{:S(2)}, u32[]{:S(2)}) collective-permute-start(bf16[80,2048]{0,1:T(8,128)(2,1)S(1)} %copy.40), channel_id=1, source_target_pairs={{62,0},{63,1},{0,2},{1,3},{2,4},{3,5},{4,6},{5,7},{6,8},{7,9},{8,1... | collective-permute-start | bytes 983048 | tf_op jit(solution)/shard_map/ppermute | solution.py:17
  69.3 101.1 %collective-permute-start.3 = (bf16[80,2048]{0,1:T(8,128)(2,1)S(1)}, bf16[80,2048]{0,1:T(8,128)(2,1)}, u32[]{:S(2)}, u32[]{:S(2)}) collective-permute-start(bf16[80,2048]{0,1:T(8,128)(2,1)S(1)} %copy.40), channel_id=1, source_target_pairs={{63,0},{0,1},{1,2},{2,3},{3,4},{4,5},{5,6},{6,7},{7,8},{8,9},{9,10... | collective-permute-start | bytes 983048 | tf_op jit(solution)/shard_map/ppermute | solution.py:17
  72.8 100.3 %collective-permute-start.4 = (bf16[80,2048]{0,1:T(8,128)(2,1)S(1)}, bf16[80,2048]{0,1:T(8,128)(2,1)}, u32[]{:S(2)}, u32[]{:S(2)}) collective-permute-start(bf16[80,2048]{0,1:T(8,128)(2,1)S(1)} %copy.40), channel_id=1, source_target_pairs={{1,0},{2,1},{3,2},{4,3},{5,4},{6,5},{7,6},{8,7},{9,8},{10,9},{11,1... | collective-permute-start | bytes 983048 | tf_op jit(solution)/shard_map/ppermute | solution.py:17
  93.8 81.2 %collective-permute-start.5 = (bf16[80,2048]{0,1:T(8,128)(2,1)S(1)}, bf16[80,2048]{0,1:T(8,128)(2,1)S(1)}, u32[]{:S(2)}, u32[]{:S(2)}) collective-permute-start(bf16[80,2048]{0,1:T(8,128)(2,1)S(1)} %copy.40), channel_id=1, source_target_pairs={{2,0},{3,1},{4,2},{5,3},{6,4},{7,5},{8,6},{9,7},{10,8},{11,9},{12,... | collective-permute-start | bytes 983048 | tf_op jit(solution)/shard_map/ppermute | solution.py:17
  116.0 114.7 %copy-start.4 = (pred[1024]{0:T(1024)(128)(4,1)S(1)}, pred[1024]{0:T(1024)(128)(4,1)}, u32[]{:S(2)}) copy-start(pred[1024]{0:T(1024)(128)(4,1)} %copy-done.3) | copy-start | bytes 3076
  140.2 51.1 %collective-permute-start.6 = (bf16[80,2048]{0,1:T(8,128)(2,1)S(1)}, bf16[80,2048]{0,1:T(8,128)(2,1)S(1)}, u32[]{:S(2)}, u32[]{:S(2)}) collective-permute-start(bf16[80,2048]{0,1:T(8,128)(2,1)S(1)} %copy.40), channel_id=1, source_target_pairs={{3,0},{4,1},{5,2},{6,3},{7,4},{8,5},{9,6},{10,7},{11,8},{12,9},{13... | collective-permute-start | bytes 983048 | tf_op jit(solution)/shard_map/ppermute | solution.py:17
  145.7 85.5 %copy-start.7 = (s32[1,1,2]{2,1,0:T(1,128)S(1)}, s32[1,1,2]{2,1,0:T(1,128)}, u32[]{:S(2)}) copy-start(s32[1,1,2]{2,1,0:T(1,128)} %param.12) | copy-start | bytes 28
  145.7 85.6 %copy-start.5 = (pred[2,512]{1,0:T(4,128)(4,1)S(1)}, pred[2,512]{1,0:T(4,128)(4,1)}, u32[]{:S(2)}) copy-start(pred[2,512]{1,0:T(4,128)(4,1)} %compare_and_fusion) | copy-start | bytes 3076
  161.9 62.2 %collective-permute-start.7 = (bf16[80,2048]{0,1:T(8,128)(2,1)S(1)}, bf16[80,2048]{0,1:T(8,128)(2,1)S(1)}, u32[]{:S(2)}, u32[]{:S(2)}) collective-permute-start(bf16[80,2048]{0,1:T(8,128)(2,1)S(1)} %copy.40), channel_id=1, source_target_pairs={{4,0},{5,1},{6,2},{7,3},{8,4},{9,5},{10,6},{11,7},{12,8},{13,9},{1... | collective-permute-start | bytes 983048 | tf_op jit(solution)/shard_map/ppermute | solution.py:17
where the time goes:
time: 290 us; the launch traced here: 289 us
  starting transfers between devices  95.1 us (33%)
  waiting for transfers between devices  92.1 us (32%)
  local copies, waits for them, and re-layouts  44.7 us (15%)
  blocking collectives  44.2 us (15%)
  matrix products  6.52 us (2%)
  other arithmetic  5.76 us (2%)
    ppermute x16, waiting for transfers between devices, from_behind(): return lax.ppermute(block, axis, route)  92.1 us
    ppermute x16, starting transfers between devices, from_behind(): return lax.ppermute(block, axis, route)  90.7 us
    psum x1, blocking collectives, body(): gram_total, drive_total = lax.psum((gram_local, drive_local), 'mem')  26.4 us
    unnamed x39, local copies, waits for them, and re-layouts  18.9 us
    all_to_all x1, blocking collectives, body(): lax.all_to_all(analysed, 'mem', split_axis=0, concat_axis=1, tiled=True)  17.8 us
    gather x1, local copies, waits for them, and re-layouts, body(): details = jnp.take(info_table, lookup, axis=1).astype(jnp.float32)  7.03 us
    gather x2, local copies, waits for them, and re-layouts, body(): columns = jnp.take(prior_table, lookup, axis=1).astype(jnp.float32)  5.95 us
  transfers between devices with their start and end apart: 17, of which 6 were waited for; matrix products, arithmetic and copies ran while one was open for 16% of the time, Pallas kernels for 0%

commit v1 on v0

v1 whole, which is shorter than its diff:
```python
import jax
import jax.numpy as jnp
from jax import lax
from jax.experimental import pallas as pl
from jax.experimental.pallas import tpu as pltpu
from jax.sharding import PartitionSpec as P

MESH = pl.DeviceIdType.MESH
F32 = jnp.float32
BF16 = jnp.bfloat16

K = 80
KLOC = 10
V = 160
NM = 8
NG = 64
NY = 4
NZ = 16
ROWS = 2048
MLOC = 512
ENT = 2 * MLOC
CAP = 128
NQ = 8
REACH = 4
ITERS = 5
TV = 16
CHUNK = 2
NCHUNK = V // (TV * CHUNK)
PARTS = ((0, 3), (3, 3), (6, 4))
KCHIP = 2 * KLOC
TABLE = 96
HALF = K // 2
PACK = HALF + 8
FARTHEST_FIRST = (3, 4, 2, 5, 1, 6, 0, 7)

NT = (((1,), (1,)), ((), ()))


def neighbour(g, q):
    offset = q + 1 if q < REACH else q + NG - 2 * REACH
    return lax.rem(g + offset, NG)


def split(x):
    high = x.astype(BF16)
    return high, (x - high.astype(F32)).astype(BF16)


def mm(a, b):
    return jnp.dot(a, b, preferred_element_type=F32)


def mm_nt(a, b):
    return lax.dot_general(a, b, NT, preferred_element_type=F32)


def mm3(a, b):
    ah, al = split(a)
    bh, bl = split(b)
    return mm(ah, bh) + (mm(ah, bl) + mm(al, bh))


def body_kernel(
    ens_ref, prior_ref, value_ref, precision_ref, ids_ref, count_ref, taper_ref, out_ref,
    table, value_v, precision_v, ids_v, taper_v, count_s,
    listed_out, req_out, req_in, resp_out, resp_in, details_out, details_in, gram, gram_in,
    states, flat, result, anomalies, means, transforms, sending,
    ready, in_sem, own_sem, ens_send, ens_recv, relay_send, req_send, req_recv, resp_send, resp_recv,
    details_send, details_recv,
    gram_send, gram_recv, out_send, out_recv, out_own,
):
    m = lax.axis_index("mem")
    g = lax.axis_index("grid")
    y, core = m // 2, lax.rem(m, 2)
    z = lax.rem(g, NZ)

    def peer(p):
        return lax.rem(m + p, NM)

    def device(dy, c):
        return lax.rem(y + dy + NY, NY) * 2 + c

    def depth_of(q):
        return lax.rem(neighbour(g, q), NZ)

    barrier = pltpu.get_barrier_semaphore()
    for q in FARTHEST_FIRST:

        @pl.when(depth_of(q) > z)
        def _():
            pl.semaphore_signal(barrier, inc=1, device_id=(m, neighbour(g, q)), device_id_type=MESH)

    for p in (4, 2, 6, 3, 5, 1, 7):
        pl.semaphore_signal(barrier, inc=1, device_id=(peer(p), g), device_id_type=MESH)
    greetings = NM - 1
    for q in range(NQ):
        greetings = greetings + (depth_of(q) < z).astype(jnp.int32)

    loads = [
        pltpu.make_async_copy(ids_ref, ids_v, in_sem.at[0]),
        pltpu.make_async_copy(taper_ref, taper_v, in_sem.at[1]),
        pltpu.make_async_copy(count_ref, count_s, in_sem.at[2]),
        pltpu.make_async_copy(value_ref, value_v, in_sem.at[3]),
        pltpu.make_async_copy(precision_ref, precision_v, in_sem.at[4]),
        pltpu.make_async_copy(prior_ref, table.at[pl.ds(0, K)], in_sem.at[5]),
    ]
    for load in loads:
        load.start()

    def block_of(ref, c):
        return ref.at[:, :, pl.ds(pl.multiple_of(c * 128, 128), 128)]

    own_states = pltpu.make_async_copy(
        block_of(ens_ref, core), states.at[pl.ds(m * KLOC, KLOC)], own_sem.at[0]
    )
    own_states.start()

    def rows_in(i):
        first, count = PARTS[i]
        return pl.ds(first * TV, count * TV)

    def states_to(i, dy, c, slot):
        return pltpu.make_async_remote_copy(
            src_ref=block_of(ens_ref, c).at[:, rows_in(i)],
            dst_ref=states.at[pl.ds(m * KLOC, KLOC), rows_in(i)],
            send_sem=ens_send.at[i, dy + 1, c],
            recv_sem=ens_recv.at[i, slot],
            device_id=(device(dy, c), g),
            device_id_type=MESH,
        )

    def states_to_sibling():
        return pltpu.make_async_remote_copy(
            src_ref=block_of(ens_ref, 1 - core),
            dst_ref=states.at[pl.ds(m * KLOC, KLOC)],
            send_sem=ens_send.at[0, 1, 0],
            recv_sem=ens_recv.at[0, 4],
            device_id=(device(0, 1 - core), g),
            device_id_type=MESH,
        )

    def hand_on(i, c):
        dy = 1 - 2 * c
        rows = pl.ds(device(-dy, c) * KLOC, KLOC)
        return pltpu.make_async_remote_copy(
            src_ref=states.at[rows, rows_in(i)],
            dst_ref=states.at[rows, rows_in(i)],
            send_sem=relay_send.at[i, c],
            recv_sem=ens_recv.at[i, 5 + c],
            device_id=(device(dy, core), g),
            device_id_type=MESH,
        )

    def relay(i):
        for c, slot in ((0, 0), (1, 3)):
            states_to(i, 1, 0, slot).wait_recv()
            hand_on(i, c).start()

    pl.semaphore_wait(barrier, greetings)
    for q in range(NQ):

        @pl.when(depth_of(q) < z)
        def _():
            pl.semaphore_signal(
                ready.at[NQ - 1 - q], inc=1, device_id=(m, neighbour(g, q)), device_id_type=MESH
            )

    for i in range(len(PARTS)):
        for c in range(2):
            for dy, slot in ((1, 0), (-1, 2)):
                states_to(i, dy, c, slot + core).start()
        if i == 0:
            states_to_sibling().start()

    for load in loads[:3]:
        load.wait()

    ids = jnp.concatenate([ids_v[0, 0, 0:1, :], ids_v[0, 0, 1:2, :]], axis=1)
    taper = jnp.concatenate([taper_v[0, 0, 0:1, :], taper_v[0, 0, 1:2, :]], axis=1)
    lane = lax.broadcasted_iota(jnp.int32, (1, ENT), 1)
    limit = jnp.where(lane < MLOC, count_s[0, 0, 0], count_s[0, 0, 1] + MLOC)
    taper = jnp.where(lane < limit, taper, 0.0)
    offset = ((ids >> 11) - g + NG) & (NG - 1)
    row = ids & (ROWS - 1)
    high = (row >> 8).astype(F32)
    low = (row & 255).astype(F32)
    bucket = jnp.where(offset <= REACH, offset - 1, offset - (NG - 2 * REACH))
    mine = bucket < 0
    named = bucket == lax.broadcasted_iota(jnp.int32, (NQ, ENT), 0)
    named_f = jnp.where(named, 1.0, 0.0)
    before = jnp.where(
        lax.broadcasted_iota(jnp.int32, (128, 128), 0)
        < lax.broadcasted_iota(jnp.int32, (128, 128), 1), 1.0, 0.0,
    ).astype(BF16)
    chunks = [named_f[:, c * 128 : (c + 1) * 128] for c in range(ENT // 128)]
    prefix = mm(jnp.concatenate(chunks, axis=0).astype(BF16), before)
    base = jnp.zeros((NQ, 1), F32)
    ranks = []
    for c, chunk in enumerate(chunks):
        ranks.append(jnp.where(chunk > 0.0, prefix[c * NQ : (c + 1) * NQ] + base, -1.0))
        base = base + jnp.sum(chunk, axis=1, keepdims=True)
    rank = jnp.concatenate(ranks, axis=1)

    t1 = taper.astype(BF16).astype(F32)
    t2 = (taper - t1).astype(BF16).astype(F32)
    t3 = taper - t1 - t2
    kind = lax.broadcasted_iota(jnp.int32, (16, ENT), 0)
    entry = lax.broadcasted_iota(jnp.int32, (16, ENT), 1)
    first_block = entry < MLOC
    listed = jnp.where(kind == 0, high, jnp.where(kind == 1, low, 0.0))
    for b in range(2):
        for i, part in enumerate((t1, t2, t3)):
            here = (kind == 2 + 3 * b + i) & (first_block if b == 0 else ~first_block)
            listed = jnp.where(here, part, listed)
    listed = listed.astype(BF16)
    slot = lax.broadcasted_iota(jnp.int32, (CAP, 256), 0).astype(F32)
    for q in range(NQ):
        total = jnp.zeros((16, CAP), F32)
        for c in range(ENT // 256):
            cols = slice(c * 256, (c + 1) * 256)
            hit = jnp.where(slot == rank[q : q + 1, cols], 1.0, 0.0).astype(BF16)
            total = total + mm_nt(listed[:, cols], hit)
        listed_out[q] = total
        req_out[q] = total[0:2]

    def request(q, back):
        return pltpu.make_async_remote_copy(
            src_ref=req_out.at[q],
            dst_ref=req_in.at[back],
            send_sem=req_send.at[q],
            recv_sem=req_recv.at[back],
            device_id=(m, neighbour(g, q)),
            device_id_type=MESH,
        )

    for q in (3, 2, 1, 0, 7, 6, 5, 4):

        @pl.when(depth_of(q) > z)
        def _():
            pl.semaphore_wait(ready.at[q], 1)

        request(q, NQ - 1 - q).start()

    relay(0)

    for load in loads[3:]:
        load.wait()
    extra = lax.broadcasted_iota(jnp.int32, (TABLE - K, ROWS), 0)
    table[K:, :] = jnp.where(
        extra == 0, value_v[...].astype(F32).reshape(1, ROWS),
        jnp.where(extra == 1, precision_v[...].astype(F32).reshape(1, ROWS), 0.0),
    ).astype(BF16)

    depth = lax.broadcasted_iota(jnp.int32, (256, 256), 0).astype(F32)

    def columns_of(high, low):
        total = jnp.zeros((TABLE, 256), F32)
        for k in range(ROWS // 256):
            wanted = jnp.where(high == k, low, -1.0)
            hit = jnp.where(depth == wanted, 1.0, 0.0).astype(BF16)
            total = total + mm(table[:, k * 256 : (k + 1) * 256], hit)
        return total

    def response(q, back):
        return pltpu.make_async_remote_copy(
            src_ref=resp_out.at[q],
            dst_ref=resp_in.at[back],
            send_sem=resp_send.at[q],
            recv_sem=resp_recv.at[back],
            device_id=(m, neighbour(g, q)),
            device_id_type=MESH,
        )

    def details(q, back):
        return pltpu.make_async_remote_copy(
            src_ref=details_out.at[q],
            dst_ref=details_in.at[back],
            send_sem=details_send.at[q],
            recv_sem=details_recv.at[back],
            device_id=(m, neighbour(g, q)),
            device_id_type=MESH,
        )

    for q, r in ((0, 7), (1, 6), (2, 5), (3, 4)):
        request(q, q).wait_recv()
        request(r, r).wait_recv()
        asked = jnp.concatenate([req_in[q], req_in[r]], axis=1)
        found = columns_of(asked[0:1], asked[1:2])
        for i, side in ((q, slice(0, CAP)), (r, slice(CAP, 2 * CAP))):
            resp_out[i] = found[:K, side].astype(BF16)
            details_out[i] = found[K : K + 2, side]
            details(i, NQ - 1 - i).start()
            response(i, NQ - 1 - i).start()

    def gram_of(columns, value, precision, weights):
        center = jnp.sum(columns, axis=0, keepdims=True) * (1.0 / K)
        deviation = columns - center
        innovation = jnp.broadcast_to(value - center, (8, columns.shape[1]))
        nothing = jnp.zeros((K, columns.shape[1]), F32)
        top_h, top_l = split(jnp.concatenate([deviation, nothing[: 128 - K]], axis=0))
        low_h, low_l = split(jnp.concatenate([nothing, deviation[HALF:], nothing[:8]], axis=0))
        grams = []
        for weight in weights:
            weight = weight * precision
            upper_h, upper_l = split(jnp.concatenate([deviation[:HALF], innovation], axis=0) * weight)
            lower_h, lower_l = split(jnp.concatenate([deviation[HALF:] * weight, nothing[:8]], axis=0))
            grams.append(
                (mm_nt(upper_h, top_h) + mm_nt(lower_h, low_h))
                + (mm_nt(upper_h, top_l) + mm_nt(lower_h, low_l))
                + (mm_nt(upper_l, top_h) + mm_nt(lower_l, low_h))
            )
        return grams

    relay(1)
    own_taper = jnp.where(mine, taper, 0.0)
    for b in range(2):
        total = jnp.zeros((PACK, 128), F32)
        for c in range(2):
            cols = slice(b * MLOC + c * 256, b * MLOC + (c + 1) * 256)
            found = columns_of(high[:, cols], low[:, cols])
            total = total + gram_of(found[:K], found[K : K + 1], found[K + 1 : K + 2], (own_taper[:, cols],))[0]
        gram[b] = total

    for q, r in ((0, 7), (1, 6), (2, 5), (3, 4)):
        for i in (q, r):
            details(i, i).wait_recv()
            response(i, i).wait_recv()
        columns = jnp.concatenate([resp_in[q], resp_in[r]], axis=1).astype(F32)
        known = jnp.concatenate([details_in[q], details_in[r]], axis=1)
        asked = jnp.concatenate([listed_out[q], listed_out[r]], axis=1)
        weights = [asked[2 + 3 * b : 3 + 3 * b] + asked[3 + 3 * b : 4 + 3 * b] + asked[4 + 3 * b : 5 + 3 * b]
                   for b in range(2)]
        for b, part in enumerate(gram_of(columns, known[0:1], known[1:2], weights)):
            gram[b] = gram[b] + part

    def gram_to(p):
        target = peer(p)
        return pltpu.make_async_remote_copy(
            src_ref=gram.at[lax.rem(target, 2)],
            dst_ref=gram_in.at[p],
            send_sem=gram_send.at[p],
            recv_sem=gram_recv.at[p],
            device_id=(target, g),
            device_id_type=MESH,
        )

    for p in range(1, NM):
        gram_to(p).start()
    relay(2)

    own_states.wait()
    states_to_sibling().wait_recv()
    def prepare(t, carry):
        x = states[:, pl.ds(pl.multiple_of(t * TV, TV), TV), :].astype(F32)
        mean = jnp.sum(x, axis=0) * (1.0 / K)
        means[t] = mean
        flat[...] = (x - mean).reshape(K * TV, 128)
        for v in range(TV):
            anomalies[t, :, v * 128 : (v + 1) * 128] = flat[pl.ds(v, K, stride=TV), :].astype(BF16)
        return carry

    def complete(i):
        for slot in (1, 2):
            states_to(i, 1, 0, slot).wait_recv()
        for c in range(2):
            hand_on(i, c).wait_recv()
        first, count = PARTS[i]
        lax.fori_loop(first, first + count, prepare, 0)

    complete(0)
    complete(1)

    total = gram[core]
    for p in range(1, NM):
        gram_to(p).wait_recv()
        total = total + gram_in[p]

    same = (lax.broadcasted_iota(jnp.int32, (K, K), 0) == lax.broadcasted_iota(jnp.int32, (K, K), 1))
    identity = jnp.where(same, 1.0, 0.0)
    drive = total[HALF : HALF + 1, :K]
    turned = jnp.transpose(total)[HALF:K, :HALF]
    corner = total[:HALF, K : K + HALF]
    gram_total = jnp.concatenate([total[:HALF, :K], jnp.concatenate([turned, corner], axis=1)], axis=0)
    system = gram_total + (K - 1.0) * identity
    scale = jnp.sqrt(jnp.sum(system * system, axis=(0, 1), keepdims=True))
    root_iter = system * (1.0 / scale)
    inverse_root = 1.5 * identity - 0.5 * root_iter
    root_iter = mm3(root_iter, inverse_root)
    for step in range(1, ITERS):
        update = 1.5 * identity - 0.5 * mm3(inverse_root, root_iter)
        if step < ITERS - 1:
            root_iter = mm3(root_iter, update)
        inverse_root = mm3(update, inverse_root)
    shift = mm3(mm3(jnp.broadcast_to(drive, (8, K)), inverse_root), inverse_root)[0:1] / scale
    transforms[...] = jnp.sqrt((K - 1.0) / scale) * inverse_root + shift
    transform = transforms[pl.ds(y * KCHIP, KCHIP), :].astype(BF16)

    def rows_of(i):
        return pl.ds(pl.multiple_of(i * (CHUNK * TV), TV), CHUNK * TV)

    def result_to_sibling(i):
        return pltpu.make_async_remote_copy(
            src_ref=sending.at[pl.ds((1 - core) * KLOC, KLOC), rows_of(i)],
            dst_ref=block_of(out_ref, core).at[:, rows_of(i)],
            send_sem=out_send.at[i],
            recv_sem=out_recv.at[i],
            device_id=(device(0, 1 - core), g),
            device_id_type=MESH,
        )

    def result_own(i):
        return pltpu.make_async_copy(
            sending.at[pl.ds(core * KLOC, KLOC), rows_of(i)],
            block_of(out_ref, core).at[:, rows_of(i)],
            out_own.at[i],
        )

    def analyse(i, carry):
        for j in range(CHUNK):
            t = i * CHUNK + j
            mean = means[t]
            moved = mm(transform, anomalies[t])
            for v in range(TV):
                result[pl.ds(v, KCHIP, stride=TV), :] = moved[:, v * 128 : (v + 1) * 128] + mean[v : v + 1]
            sending[:, pl.ds(pl.multiple_of(t * TV, TV), TV), :] = (
                result[...].reshape(KCHIP, TV, 128).astype(BF16)
            )
        result_to_sibling(i).start()
        result_own(i).start()
        return carry

    lax.fori_loop(0, PARTS[2][0] // CHUNK, analyse, 0)
    complete(2)
    lax.fori_loop(PARTS[2][0] // CHUNK, NCHUNK, analyse, 0)

    for i in range(NCHUNK):
        result_to_sibling(i).wait_recv()
        result_to_sibling(i).wait_send()
        result_own(i).wait()
    for i in range(len(PARTS)):
        for c in range(2):
            for dy in (1, -1):
                states_to(i, dy, c, 0).wait_send()
            hand_on(i, c).wait_send()
    states_to_sibling().wait_send()
    for p in range(1, NM):
        gram_to(p).wait_send()

    for q in range(NQ):
        request(q, NQ - 1 - q).wait_send()
        response(q, NQ - 1 - q).wait_send()
        details(q, NQ - 1 - q).wait_send()


def body(ensemble, obs_prior, obs_value, obs_precision, entry_ids, entry_count, entry_taper):
    hbm = pl.BlockSpec(memory_space=pltpu.HBM)
    dma = pltpu.SemaphoreType.DMA
    return pl.pallas_call(
        body_kernel,
        out_shape=jax.ShapeDtypeStruct(ensemble.shape, ensemble.dtype),
        in_specs=[hbm] * 7,
        out_specs=hbm,
        scratch_shapes=[
            pltpu.VMEM((TABLE, ROWS), BF16),
            pltpu.VMEM((ROWS,), BF16),
            pltpu.VMEM((ROWS,), BF16),
            pltpu.VMEM((1, 1, 2, MLOC), jnp.int32),
            pltpu.VMEM((1, 1, 2, MLOC), F32),
            pltpu.SMEM((1, 1, 2), jnp.int32),
            pltpu.VMEM((NQ, 16, CAP), F32),
            pltpu.VMEM((NQ, 2, CAP), F32),
            pltpu.VMEM((NQ, 2, CAP), F32),
            pltpu.VMEM((NQ, K, CAP), BF16),
            pltpu.VMEM((NQ, K, CAP), BF16),
            pltpu.VMEM((NQ, 2, CAP), F32),
            pltpu.VMEM((NQ, 2, CAP), F32),
            pltpu.VMEM((2, PACK, 128), F32),
            pltpu.VMEM((NM, PACK, 128), F32),
            pltpu.VMEM((K, V, 128), BF16),
            pltpu.VMEM((K * TV, 128), F32),
            pltpu.VMEM((KCHIP * TV, 128), F32),
            pltpu.VMEM((V // TV, K, TV * 128), BF16),
            pltpu.VMEM((V // TV, TV, 128), F32),
            pltpu.VMEM((K, K), F32),
            pltpu.VMEM((KCHIP, V, 128), BF16),
            pltpu.SemaphoreType.REGULAR((NQ,)),
            dma((6,)),
            dma((1,)),
            dma((3, 3, 2)),
            dma((3, 7)),
            dma((3, 2)),
            dma((NQ,)),
            dma((NQ,)),
            dma((NQ,)),
            dma((NQ,)),
            dma((NQ,)),
            dma((NQ,)),
            dma((NM,)),
            dma((NM,)),
            dma((NCHUNK,)),
            dma((NCHUNK,)),
            dma((NCHUNK,)),
        ],
        compiler_params=pltpu.CompilerParams(
            collective_id=0, has_side_effects=True, vmem_limit_bytes=60 * 1024 * 1024
        ),
        name="analysis",
    )(ensemble, obs_prior, obs_value, obs_precision, entry_ids, entry_count, entry_taper)


def solution(mesh):
    return jax.shard_map(
        body,
        mesh=mesh,
        in_specs=(
            P("mem", None, "grid"),
            P(None, ("mem", "grid")),
            P(("mem", "grid")),
            P(("mem", "grid")),
            P("mem", "grid", None, None),
            P("mem", "grid", None),
            P("mem", "grid", None, None),
        ),
        out_specs=P("mem", None, "grid"),
        check_vma=False,
    )
```

time: 290 us -> 47.4 us (0.16)
  the two profiles are of different devices: /device:TPU:32 before, /device:TPU:1 now
where the time goes in v1:
time: 47.4 us; the launch traced here: 47.2 us
  Pallas kernels  45.1 us (95%)
  local copies, waits for them, and re-layouts  2.09 us (4%)
    pallas_call x1, Pallas kernels, body(): pl.pallas_call(body_kernel, out_shape=jax.ShapeDtypeStruct(ensemble.shape...  45.1 us
    unnamed x1, local copies, waits for them, and re-layouts  2.09 us

profile of v1, /device:TPU:1, one launch (start us, length us, event | category | flops | bytes accessed | tf_op | source)
XLA Modules:
  0.0 47.2 jit_solution(15147131817975285104)
XLA Ops:
  0.0 45.1 %analysis.1 = bf16[10,160,256]{2,1,0:T(8,128)(2,1)} custom-call(bf16[10,160,256]{2,1,0:T(8,128)(2,1)} %ens_ref.1, bf16[80,2048]{1,0:T(8,128)(2,1)} %prior_ref.1, bf16[2048]{0:T(1024)(128)(2,1)} %value_ref.1, bf16[2048]{0:T(1024)(128)(2,1)} %precision_ref.1, s32[1,1,2,512]{3,2,1,0:T(2,128)} %ids_ref.1, s32[1,1,2]{2,1,0:T(1,128)} %count_ref.1, ...), custom_call_target="tpu_custom_call" | custom-call | tf_op jit(solution)/shard_map/analysis/pallas_call | solution.py:458
  45.1 2.1 %copy.9 = bf16[10,160,256]{2,1,0:T(8,128)(2,1)} copy(bf16[10,160,256]{2,1,0:T(8,128)(2,1)} %analysis.1) | data formatting | bytes 1638400

commit v2 on v1

--- a/solution.py
+++ b/solution.py
@@ -24,8 +24,7 @@
 REACH = 4
 ITERS = 5
 TV = 16
-CHUNK = 2
-NCHUNK = V // (TV * CHUNK)
+TILES = V // TV
 PARTS = ((0, 3), (3, 3), (6, 4))
 KCHIP = 2 * KLOC
 TABLE = 96
@@ -57,14 +56,18 @@
 def mm3(a, b):
     ah, al = split(a)
     bh, bl = split(b)
-    return mm(ah, bh) + (mm(ah, bl) + mm(al, bh))
+    halves = jnp.concatenate([bh, bl], axis=1)
+    halves = jnp.concatenate([halves, jnp.zeros((128 - K, 256), BF16)], axis=0)
+    rows = a.shape[0]
+    parts = mm(jnp.concatenate([ah, al], axis=0), halves)
+    return parts[:rows, :128] + (parts[:rows, 128:] + parts[rows:, :128])
 
 
 def body_kernel(
     ens_ref, prior_ref, value_ref, precision_ref, ids_ref, count_ref, taper_ref, out_ref,
     table, value_v, precision_v, ids_v, taper_v, count_s,
     listed_out, req_out, req_in, resp_out, resp_in, details_out, details_in, gram, gram_in,
-    states, flat, result, anomalies, means, transforms, sending,
+    states, result, anomalies, means, transforms, sending,
     ready, in_sem, own_sem, ens_send, ens_recv, relay_send, req_send, req_recv, resp_send, resp_recv,
     details_send, details_recv,
     gram_send, gram_recv, out_send, out_recv, out_own,
@@ -157,7 +160,7 @@
             hand_on(i, c).start()
 
     pl.semaphore_wait(barrier, greetings)
-    for q in range(NQ):
+    for q in FARTHEST_FIRST:
 
         @pl.when(depth_of(q) < z)
         def _():
@@ -344,7 +347,7 @@
             device_id_type=MESH,
         )
 
-    for p in range(1, NM):
+    for p in (4, 3, 5, 2, 6, 1, 7):
         gram_to(p).start()
     relay(2)
 
@@ -354,9 +357,9 @@
         x = states[:, pl.ds(pl.multiple_of(t * TV, TV), TV), :].astype(F32)
         mean = jnp.sum(x, axis=0) * (1.0 / K)
         means[t] = mean
-        flat[...] = (x - mean).reshape(K * TV, 128)
+        turned = jnp.swapaxes(x - mean, 0, 1)
         for v in range(TV):
-            anomalies[t, :, v * 128 : (v + 1) * 128] = flat[pl.ds(v, K, stride=TV), :].astype(BF16)
+            anomalies[t, :, v * 128 : (v + 1) * 128] = turned[v].astype(BF16)
         return carry
 
     def complete(i):
@@ -375,13 +378,15 @@
         gram_to(p).wait_recv()
         total = total + gram_in[p]
 
-    same = (lax.broadcasted_iota(jnp.int32, (K, K), 0) == lax.broadcasted_iota(jnp.int32, (K, K), 1))
+    same = lax.broadcasted_iota(jnp.int32, (K, 128), 0) == lax.broadcasted_iota(jnp.int32, (K, 128), 1)
     identity = jnp.where(same, 1.0, 0.0)
-    drive = total[HALF : HALF + 1, :K]
+    drive = total[HALF : HALF + 1]
     turned = jnp.transpose(total)[HALF:K, :HALF]
     corner = total[:HALF, K : K + HALF]
-    gram_total = jnp.concatenate([total[:HALF, :K], jnp.concatenate([turned, corner], axis=1)], axis=0)
-    system = gram_total + (K - 1.0) * identity
+    lower = jnp.concatenate([turned, corner, jnp.zeros((HALF, 128 - K), F32)], axis=1)
+    inside = lax.broadcasted_iota(jnp.int32, (HALF, 128), 1) < K
+    upper = jnp.where(inside, total[:HALF], 0.0)
+    system = jnp.concatenate([upper, lower], axis=0) + (K - 1.0) * identity
     scale = jnp.sqrt(jnp.sum(system * system, axis=(0, 1), keepdims=True))
     root_iter = system * (1.0 / scale)
     inverse_root = 1.5 * identity - 0.5 * root_iter
@@ -391,12 +396,12 @@
         if step < ITERS - 1:
             root_iter = mm3(root_iter, update)
         inverse_root = mm3(update, inverse_root)
-    shift = mm3(mm3(jnp.broadcast_to(drive, (8, K)), inverse_root), inverse_root)[0:1] / scale
+    shift = mm3(mm3(jnp.broadcast_to(drive, (16, 128)), inverse_root), inverse_root)[0:1] / scale
     transforms[...] = jnp.sqrt((K - 1.0) / scale) * inverse_root + shift
-    transform = transforms[pl.ds(y * KCHIP, KCHIP), :].astype(BF16)
+    transform = transforms[pl.ds(y * KCHIP, KCHIP), :][:, :K].astype(BF16)
 
     def rows_of(i):
-        return pl.ds(pl.multiple_of(i * (CHUNK * TV), TV), CHUNK * TV)
+        return pl.ds(pl.multiple_of(i * TV, TV), TV)
 
     def result_to_sibling(i):
         return pltpu.make_async_remote_copy(
@@ -415,25 +420,22 @@
             out_own.at[i],
         )
 
-    def analyse(i, carry):
-        for j in range(CHUNK):
-            t = i * CHUNK + j
-            mean = means[t]
-            moved = mm(transform, anomalies[t])
-            for v in range(TV):
-                result[pl.ds(v, KCHIP, stride=TV), :] = moved[:, v * 128 : (v + 1) * 128] + mean[v : v + 1]
-            sending[:, pl.ds(pl.multiple_of(t * TV, TV), TV), :] = (
-                result[...].reshape(KCHIP, TV, 128).astype(BF16)
-            )
-        result_to_sibling(i).start()
-        result_own(i).start()
+    def analyse(t, carry):
+        moved = mm(transform, anomalies[t])
+        mean = means[t]
+        for v in range(TV):
+            result[pl.ds(v, KCHIP, stride=TV), :] = moved[:, v * 128 : (v + 1) * 128] + mean[v : v + 1]
+        sending[:, rows_of(t), :] = result[...].reshape(KCHIP, TV, 128).astype(BF16)
+        result_to_sibling(t).start()
+        result_own(t).start()
         return carry
 
-    lax.fori_loop(0, PARTS[2][0] // CHUNK, analyse, 0)
+    late = PARTS[2][0]
+    lax.fori_loop(0, late, analyse, 0)
     complete(2)
-    lax.fori_loop(PARTS[2][0] // CHUNK, NCHUNK, analyse, 0)
-
-    for i in range(NCHUNK):
+    lax.fori_loop(late, TILES, analyse, 0)
+
+    for i in range(TILES):
         result_to_sibling(i).wait_recv()
         result_to_sibling(i).wait_send()
         result_own(i).wait()
@@ -457,9 +459,9 @@
     dma = pltpu.SemaphoreType.DMA
     return pl.pallas_call(
         body_kernel,
-        out_shape=jax.ShapeDtypeStruct(ensemble.shape, ensemble.dtype),
+        out_shape=pltpu.VMEM(ensemble.shape, ensemble.dtype),
         in_specs=[hbm] * 7,
-        out_specs=hbm,
+        out_specs=pl.BlockSpec(memory_space=pltpu.VMEM),
         scratch_shapes=[
             pltpu.VMEM((TABLE, ROWS), BF16),
             pltpu.VMEM((ROWS,), BF16),
@@ -477,11 +479,10 @@
             pltpu.VMEM((2, PACK, 128), F32),
             pltpu.VMEM((NM, PACK, 128), F32),
             pltpu.VMEM((K, V, 128), BF16),
-            pltpu.VMEM((K * TV, 128), F32),
             pltpu.VMEM((KCHIP * TV, 128), F32),
             pltpu.VMEM((V // TV, K, TV * 128), BF16),
             pltpu.VMEM((V // TV, TV, 128), F32),
-            pltpu.VMEM((K, K), F32),
+            pltpu.VMEM((K, 128), F32),
             pltpu.VMEM((KCHIP, V, 128), BF16),
             pltpu.SemaphoreType.REGULAR((NQ,)),
             dma((6,)),
@@ -497,9 +498,9 @@
             dma((NQ,)),
             dma((NM,)),
             dma((NM,)),
-            dma((NCHUNK,)),
-            dma((NCHUNK,)),
-            dma((NCHUNK,)),
+            dma((TILES,)),
+            dma((TILES,)),
+            dma((TILES,)),
         ],
         compiler_params=pltpu.CompilerParams(
             collective_id=0, has_side_effects=True, vmem_limit_bytes=60 * 1024 * 1024

time: 47.4 us -> 46.6 us (0.983)
  local copies, waits for them, and re-layouts: 2.09 us -> 0.89 us
    unnamed x1, local copies, waits for them, and re-layouts: 2.09 us -> 0.89 us
where the time goes in v2:
time: 46.6 us; the launch traced here: 46.4 us
  Pallas kernels  45.5 us (98%)
  local copies, waits for them, and re-layouts  0.89 us (2%)
    pallas_call x1, Pallas kernels, body(): pl.pallas_call(body_kernel, out_shape=pltpu.VMEM(ensemble.shape, ensemble...  45.5 us

profile of v2, /device:TPU:1, one launch (start us, length us, event | category | flops | bytes accessed | tf_op | source)
XLA Modules:
  0.0 46.4 jit_solution(18305126165682810961)
XLA Ops:
  0.0 45.5 %analysis.1 = bf16[10,160,256]{2,1,0:T(8,128)(2,1)S(1)} custom-call(bf16[10,160,256]{2,1,0:T(8,128)(2,1)} %ens_ref.1, bf16[80,2048]{1,0:T(8,128)(2,1)} %prior_ref.1, bf16[2048]{0:T(1024)(128)(2,1)} %value_ref.1, bf16[2048]{0:T(1024)(128)(2,1)} %precision_ref.1, s32[1,1,2,512]{3,2,1,0:T(2,128)} %ids_ref.1, s32[1,1,2]{2,1,0:T(1,128)} %count_ref.1, ...), custom_call_target="tpu_custom_call" | custom-call | tf_op jit(solution)/shard_map/analysis/pallas_call | solution.py:460
  45.5 0.9 %copy.9 = bf16[10,160,256]{2,1,0:T(8,128)(2,1)} copy(bf16[10,160,256]{2,1,0:T(8,128)(2,1)S(1)} %analysis.1) | data formatting | bytes 1638400

commit v3 on v2

--- a/solution.py
+++ b/solution.py
@@ -244,8 +244,6 @@
 
         request(q, NQ - 1 - q).start()
 
-    relay(0)
-
     for load in loads[3:]:
         load.wait()
     extra = lax.broadcasted_iota(jnp.int32, (TABLE - K, ROWS), 0)
@@ -314,6 +312,7 @@
             )
         return grams
 
+    relay(0)
     relay(1)
     own_taper = jnp.where(mine, taper, 0.0)
     for b in range(2):
@@ -368,7 +367,14 @@
         for c in range(2):
             hand_on(i, c).wait_recv()
         first, count = PARTS[i]
-        lax.fori_loop(first, first + count, prepare, 0)
+        step = 2 if count % 2 == 0 else 1
+
+        def several(k, carry):
+            for j in range(step):
+                prepare(first + step * k + j, carry)
+            return carry
+
+        lax.fori_loop(0, count // step, several, 0)
 
     complete(0)
     complete(1)
@@ -397,7 +403,7 @@
             root_iter = mm3(root_iter, update)
         inverse_root = mm3(update, inverse_root)
     shift = mm3(mm3(jnp.broadcast_to(drive, (16, 128)), inverse_root), inverse_root)[0:1] / scale
-    transforms[...] = jnp.sqrt((K - 1.0) / scale) * inverse_root + shift
+    transforms[:K] = jnp.sqrt((K - 1.0) / scale) * inverse_root + shift
     transform = transforms[pl.ds(y * KCHIP, KCHIP), :][:, :K].astype(BF16)
 
     def rows_of(i):
@@ -420,20 +426,24 @@
             out_own.at[i],
         )
 
-    def analyse(t, carry):
-        moved = mm(transform, anomalies[t])
-        mean = means[t]
-        for v in range(TV):
-            result[pl.ds(v, KCHIP, stride=TV), :] = moved[:, v * 128 : (v + 1) * 128] + mean[v : v + 1]
-        sending[:, rows_of(t), :] = result[...].reshape(KCHIP, TV, 128).astype(BF16)
-        result_to_sibling(t).start()
-        result_own(t).start()
-        return carry
+    def analyse(first, count):
+        for j in range(count):
+            t = first + j
+            moved = mm(transform, anomalies[t])
+            mean = means[t]
+            for v in range(TV):
+                result[j, pl.ds(v, KCHIP, stride=TV), :] = moved[:, v * 128 : (v + 1) * 128] + mean[v : v + 1]
+        for j in range(count):
+            t = first + j
+            sending[:, t * TV : (t + 1) * TV, :] = result[j, : KCHIP * TV].reshape(KCHIP, TV, 128).astype(BF16)
+            result_to_sibling(t).start()
+            result_own(t).start()
 
     late = PARTS[2][0]
-    lax.fori_loop(0, late, analyse, 0)
+    analyse(0, 3)
+    analyse(3, 3)
     complete(2)
-    lax.fori_loop(late, TILES, analyse, 0)
+    analyse(6, 4)
 
     for i in range(TILES):
         result_to_sibling(i).wait_recv()
@@ -470,19 +480,19 @@
             pltpu.VMEM((1, 1, 2, MLOC), F32),
             pltpu.SMEM((1, 1, 2), jnp.int32),
             pltpu.VMEM((NQ, 16, CAP), F32),
-            pltpu.VMEM((NQ, 2, CAP), F32),
+            pltpu.VMEM((NQ + 4, 2, CAP), F32),
             pltpu.VMEM((NQ, 2, CAP), F32),
             pltpu.VMEM((NQ, K, CAP), BF16),
             pltpu.VMEM((NQ, K, CAP), BF16),
-            pltpu.VMEM((NQ, 2, CAP), F32),
+            pltpu.VMEM((NQ + 4, 2, CAP), F32),
             pltpu.VMEM((NQ, 2, CAP), F32),
             pltpu.VMEM((2, PACK, 128), F32),
             pltpu.VMEM((NM, PACK, 128), F32),
             pltpu.VMEM((K, V, 128), BF16),
-            pltpu.VMEM((KCHIP * TV, 128), F32),
+            pltpu.VMEM((4, 24 * TV, 128), F32),
             pltpu.VMEM((V // TV, K, TV * 128), BF16),
             pltpu.VMEM((V // TV, TV, 128), F32),
-            pltpu.VMEM((K, 128), F32),
+            pltpu.VMEM((K + 8, 128), F32),
             pltpu.VMEM((KCHIP, V, 128), BF16),
             pltpu.SemaphoreType.REGULAR((NQ,)),
             dma((6,)),

time: 46.6 us -> 45.4 us (0.974)
  Pallas kernels: 45.5 us -> 44.4 us
    pallas_call x1, Pallas kernels: 45.5 us -> 44.4 us  [body(): pl.pallas_call(body_kernel, out_shape=pltpu.VMEM(ensemble.shape, ensemble...]
where the time goes in v3:
time: 45.4 us; the launch traced here: 45.3 us
  Pallas kernels  44.4 us (98%)
  local copies, waits for them, and re-layouts  0.89 us (2%)
    pallas_call x1, Pallas kernels, body(): pl.pallas_call(body_kernel, out_shape=pltpu.VMEM(ensemble.shape, ensemble...  44.4 us

profile of v3, /device:TPU:1, one launch (start us, length us, event | category | flops | bytes accessed | tf_op | source)
XLA Modules:
  0.0 45.3 jit_solution(5109966973878684506)
XLA Ops:
  0.0 44.4 %analysis.1 = bf16[10,160,256]{2,1,0:T(8,128)(2,1)S(1)} custom-call(bf16[10,160,256]{2,1,0:T(8,128)(2,1)} %ens_ref.1, bf16[80,2048]{1,0:T(8,128)(2,1)} %prior_ref.1, bf16[2048]{0:T(1024)(128)(2,1)} %value_ref.1, bf16[2048]{0:T(1024)(128)(2,1)} %precision_ref.1, s32[1,1,2,512]{3,2,1,0:T(2,128)} %ids_ref.1, s32[1,1,2]{2,1,0:T(1,128)} %count_ref.1, ...), custom_call_target="tpu_custom_call" | custom-call | tf_op jit(solution)/shard_map/analysis/pallas_call | solution.py:470
  44.4 0.9 %copy.9 = bf16[10,160,256]{2,1,0:T(8,128)(2,1)} copy(bf16[10,160,256]{2,1,0:T(8,128)(2,1)S(1)} %analysis.1) | data formatting | bytes 1638400

commit v4 on v3

--- a/solution.py
+++ b/solution.py
@@ -443,7 +443,8 @@
     analyse(0, 3)
     analyse(3, 3)
     complete(2)
-    analyse(6, 4)
+    analyse(6, 2)
+    analyse(8, 2)
 
     for i in range(TILES):
         result_to_sibling(i).wait_recv()

time: 45.4 us -> 45.4 us (level)
  no operation moved by 1% of the time
where the time goes in v4:
time: 45.4 us; the launch traced here: 45.3 us
  Pallas kernels  44.4 us (98%)
  local copies, waits for them, and re-layouts  0.89 us (2%)
    pallas_call x1, Pallas kernels, body(): pl.pallas_call(body_kernel, out_shape=pltpu.VMEM(ensemble.shape, ensemble...  44.4 us

profile of v4, /device:TPU:1, one launch (start us, length us, event | category | flops | bytes accessed | tf_op | source)
XLA Modules:
  0.0 45.3 jit_solution(9443000010269865644)
XLA Ops:
  0.0 44.4 %analysis.1 = bf16[10,160,256]{2,1,0:T(8,128)(2,1)S(1)} custom-call(bf16[10,160,256]{2,1,0:T(8,128)(2,1)} %ens_ref.1, bf16[80,2048]{1,0:T(8,128)(2,1)} %prior_ref.1, bf16[2048]{0:T(1024)(128)(2,1)} %value_ref.1, bf16[2048]{0:T(1024)(128)(2,1)} %precision_ref.1, s32[1,1,2,512]{3,2,1,0:T(2,128)} %ids_ref.1, s32[1,1,2]{2,1,0:T(1,128)} %count_ref.1, ...), custom_call_target="tpu_custom_call" | custom-call | tf_op jit(solution)/shard_map/analysis/pallas_call | solution.py:471
  44.4 0.9 %copy.9 = bf16[10,160,256]{2,1,0:T(8,128)(2,1)} copy(bf16[10,160,256]{2,1,0:T(8,128)(2,1)S(1)} %analysis.1) | data formatting | bytes 1638400
